TPU v7x, 32 devices: a whole 2x2x4 slice. The times are simulated.
32 devices in a mesh: ctx: 8 (over z, y), head: 4 (over x, core).
Axes of the slice: x: 2, y: 2, z: 4, core: 2. Of those that a mesh axis runs over, the one named last changes fastest.
Arguments:
- latents: float32 [512, 1024], replicated, may hold values from -5 to 5
- observations: float32 [16384, 1024], P('ctx'), may hold values from -45 to 45
- w_query: float32 [1024, 1024], P(None, 'head'), as said below
- w_key: float32 [1024, 1024], P(None, 'head'), as said below
- w_value: float32 [1024, 1024], P(None, 'head'), may hold values from -0.1875 to 0.1875
- w_out: float32 [1024, 1024], P('head'), may hold values from -0.1875 to 0.1875
- d_out: float32 [512, 1024], replicated, may hold values from -6 to 6
Outputs:
- d_latents: float32 [512, 1024], P(None, 'head')
- d_observations: float32 [16384, 1024], P('ctx', 'head')
- d_w_query: float32 [1024, 1024], P(None, 'head')
- d_w_key: float32 [1024, 1024], P('ctx', 'head')
- d_w_value: float32 [1024, 1024], P('ctx', 'head')
- d_w_out: float32 [1024, 1024], P('head')
Inputs may be any that keep to these rules, and one draw needn't show every extreme that they name: `w_query`: every entry lies within -5 / sqrt(1024) to 5 / sqrt(1024). `w_key`: every entry lies within -7 / sqrt(1024) to 7 / sqrt(1024).
All inputs are finite; a program needn't handle non-finite values.
Results may differ from a plain program's by a relative error of at most 0.0003.
Values sent between devices are 32-bit elements; how exact they have to be, the bound alone decides.
A program may use at most 128 MiB of HBM per device.

v0:
```python
import functools
import math

import jax
import jax.numpy as jnp
from jax import lax
from jax.experimental import pallas as pl
from jax.experimental.pallas import tpu as pltpu
from jax.sharding import PartitionSpec as P

DH = 128
CORES = 2
F32 = jnp.float32
BF16 = jnp.bfloat16
MESH = pl.DeviceIdType.MESH
STD = (((1,), (0,)), ((), ()))
RHS_T = (((1,), (1,)), ((), ()))


def split(x):
    hi = x.astype(BF16)
    return hi, (x - hi.astype(F32)).astype(BF16)


def dot(a, b, dims=STD):
    return lax.dot_general(a, b, dims, preferred_element_type=F32)


def dot3(a, b, dims=STD):
    (ah, al), (bh, bl) = a, b
    return dot(ah, bh, dims) + (dot(ah, bl, dims) + dot(al, bh, dims))


def wide_left(x):
    hi, lo = split(x)
    return jnp.concatenate([hi, hi, lo, lo], axis=1)


def wide_right(x):
    hi, lo = split(x)
    return jnp.concatenate([hi, lo, hi, lo], axis=1)


def narrow_dot(a, b_pair, b_hi):
    hi, lo = split(a)
    both = dot(hi, b_pair)
    return both[:, :DH] + (both[:, DH:] + dot(lo, b_hi))


def short_dot(a_t, b):
    ah, al = split(a_t)
    bh, bl = split(b)
    both = dot(jnp.concatenate([ah, al], axis=0), bh)
    return both[:DH] + (both[DH:] + dot(ah, bl))


def kernel(
    cfg,
    lat, obs, wq, wk, wv, wo, dout,
    dlat_o, dobs_o, dwq_o, dwk_o, dwv_o, dwo_o,
    expo, dprob, kv, obuf, wh, wl, q4, g4, qp, gp, stat, rstat, acc,
    one_recv, x_recv,
    dw, dw1, dw2, ab, ab1, ab2, db, db1, db2, aall, dall, lall, wqr, hbuf,
    obs_sem, st_s, st_r, wq_s, wq_r, h_s, h_r, t1_s, t1_r, tx_s, tx_r,
    y_s, y_r, z_s, z_r,
):
    NC, NH, NY, TC = cfg
    NZ, NX = NC // NY, NH // CORES
    T, D = obs.shape
    L, W = lat.shape[0], wq.shape[1]
    H, NCH, blk, la = W // DH, T // TC, D // NH, L // NC
    scale = 1.0 / math.sqrt(DH)
    ctx, head = lax.axis_index("ctx"), lax.axis_index("head")
    z, y = ctx // NY, lax.rem(ctx, NY)
    x, core = head // CORES, lax.rem(head, CORES)

    def other(me, k, n):
        return lax.rem(me + k, n)

    barrier = pltpu.get_barrier_semaphore()
    for k in range(1, NC):
        pl.semaphore_signal(barrier, inc=1, device_id=(other(ctx, k, NC), head), device_id_type=MESH)
    for k in range(1, NH):
        pl.semaphore_signal(barrier, inc=1, device_id=(ctx, other(head, k, NH)), device_id_type=MESH)

    def fetch(i):
        s = lax.rem(i, 2)
        return pltpu.make_async_copy(obs.at[pl.ds(pl.multiple_of(i * TC, TC), TC)], obuf.at[s], obs_sem.at[s])

    def remote(src, dst, ss, rs, dev):
        return pltpu.make_async_remote_copy(
            src_ref=src, dst_ref=dst, send_sem=ss, recv_sem=rs, device_id=dev, device_id_type=MESH
        )

    fetch(0).start()
    for half, w in ((0, wk), (1, wv)):
        hi, lo = split(w[...])
        wh[:, half * W:(half + 1) * W] = hi
        wl[:, half * W:(half + 1) * W] = lo
    q = dot3(split(lat[...]), split(wq[...])) * scale
    g = dot3(split(dout[...]), split(wo[...]), RHS_T)
    for h in range(H):
        for full, wide, pair in ((q, q4, qp), (g, g4, gp)):
            piece = full[:, h * DH:(h + 1) * DH]
            wide[h] = wide_right(piece)
            pair[h] = jnp.concatenate(split(piece), axis=1)
    pl.semaphore_wait(barrier, NC + NH - 2)

    wq_copies = [
        remote(
            wq.at[pl.ds(pl.multiple_of(other(head, k, NH) * blk, blk), blk)], wqr.at[k],
            wq_s.at[k], wq_r.at[k], (ctx, other(head, k, NH)),
        )
        for k in range(1, NH)
    ]
    for c in wq_copies:
        c.start()

    def rows(i):
        return pl.ds(pl.multiple_of(i * TC, TC), TC)

    def scores_step(i, tops):
        @pl.when(i + 1 < NCH)
        def _():
            fetch(i + 1).start()

        fetch(i).wait()
        o = split(obuf[lax.rem(i, 2)])
        both = dot3(o, (wh[...], wl[...]))
        kv[i] = both
        out = []
        for h in range(H):
            s = dot(wide_left(both[:, h * DH:(h + 1) * DH]), q4[h], RHS_T)
            expo[h, rows(i)] = s
            out.append(jnp.maximum(tops[h], jnp.max(s, axis=0, keepdims=True)))
            dprob[h, rows(i)] = dot(wide_left(both[:, W + h * DH:W + (h + 1) * DH]), g4[h], RHS_T)
        return tuple(out)

    tops = lax.fori_loop(0, NCH, scores_step, tuple(jnp.full((1, L), -3e38, F32) for _ in range(H)))
    fetch(0).start()

    def exp_step(i, sums):
        out = []
        for h in range(H):
            e = jnp.exp(expo[h, rows(i)] - tops[h])
            expo[h, rows(i)] = e
            out.append(sums[2 * h] + jnp.sum(e, axis=0, keepdims=True))
            out.append(sums[2 * h + 1] + jnp.sum(e * dprob[h, rows(i)], axis=0, keepdims=True))
        return tuple(out)

    sums = lax.fori_loop(0, NCH, exp_step, tuple(jnp.zeros((1, L), F32) for _ in range(2 * H)))
    stat[...] = jnp.zeros_like(stat)
    for h in range(H):
        stat[3 * h:3 * h + 1] = tops[h]
        stat[3 * h + 1:3 * h + 2] = sums[2 * h]
        stat[3 * h + 2:3 * h + 3] = sums[2 * h + 1]
    st_copies = [
        remote(stat, rstat.at[k], st_s.at[k], st_r.at[k], (other(ctx, k, NC), head)) for k in range(1, NC)
    ]
    for c in st_copies:
        c.start()

    acc[...] = jnp.zeros_like(acc)

    def acc_step(i, _):
        both = kv[i]
        for h in range(H):
            v_t = both[:, W + h * DH:W + (h + 1) * DH].T
            acc[h * DH:(h + 1) * DH] += short_dot(v_t, expo[h, rows(i)])
        return 0

    lax.fori_loop(0, NCH, acc_step, 0)

    for c in st_copies:
        c.wait()
    weights, deltas = [], []
    for h in range(H):
        top = tops[h]
        for k in range(1, NC):
            top = jnp.maximum(top, rstat[k, 3 * h:3 * h + 1])
        mine = jnp.exp(tops[h] - top)
        total, cross = mine * sums[2 * h], mine * sums[2 * h + 1]
        for k in range(1, NC):
            theirs = jnp.exp(rstat[k, 3 * h:3 * h + 1] - top)
            total += theirs * rstat[k, 3 * h + 1:3 * h + 2]
            cross += theirs * rstat[k, 3 * h + 2:3 * h + 3]
        weights.append(mine / total)
        deltas.append(cross / total)

    def sum_y(buf, got, n):
        return [
            remote(buf.at[:, other(y, k, NY)], got.at[k], y_s.at[n, k], y_r.at[n, k], (z * NY + other(y, k, NY), head))
            for k in range(1, NY)
        ]

    def sum_z(buf, got, n):
        return [
            remote(buf.at[other(z, k, NZ), y], got.at[k], z_s.at[n, k], z_r.at[n, k], (other(z, k, NZ) * NY + y, head))
            for k in range(1, NZ)
        ]

    def all_z(buf, n):
        return [
            remote(buf.at[z, y], buf.at[z, y], z_s.at[n, k], z_r.at[n, k], (other(z, k, NZ) * NY + y, head))
            for k in range(1, NZ)
        ]

    def all_y(buf, n):
        return [
            remote(buf.at[:, y], buf.at[:, y], y_s.at[n, k], y_r.at[n, k], (z * NY + other(y, k, NY), head))
            for k in range(1, NY)
        ]

    def start(copies):
        for c in copies:
            c.start()
        return copies

    def wait(copies):
        for c in copies:
            c.wait()

    def add_y(buf, got):
        total = buf[:, pl.ds(y, 1)]
        for k in range(1, NY):
            total += got[k].reshape(total.shape)
        buf[:, pl.ds(y, 1)] = total

    def add_z(buf, got):
        total = buf[pl.ds(z, 1), pl.ds(y, 1)].reshape(got.shape[1:])
        for k in range(1, NZ):
            total += got[k]
        return total

    def put(buf, value):
        buf[pl.ds(z, 1), pl.ds(y, 1)] = value.reshape((1, 1) + value.shape)

    for h in range(H):
        ab[:, :, :, h * DH:(h + 1) * DH] = (acc[h * DH:(h + 1) * DH] * weights[h]).T.reshape(NZ, NY, la, DH)
    att_y = start(sum_y(ab, ab1, 0))

    acc[...] = jnp.zeros_like(acc)
    dw[...] = jnp.zeros_like(dw)

    def grad_step(i, _):
        @pl.when(i + 1 < NCH)
        def _():
            fetch(i + 1).start()

        fetch(i).wait()
        both = kv[i]
        dk, dv = [], []
        for h in range(H):
            p = expo[h, rows(i)] * weights[h]
            ds = p * (dprob[h, rows(i)] - deltas[h])
            dk.append(narrow_dot(ds, qp[h], qp[h, :, :DH]))
            dv.append(narrow_dot(p, gp[h], gp[h, :, :DH]))
            acc[h * DH:(h + 1) * DH] += short_dot(both[:, h * DH:(h + 1) * DH].T, ds)
        both = jnp.concatenate(dk + dv, axis=1)
        kv[i] = both
        o_t = obuf[lax.rem(i, 2)].T
        dw[...] += dot3(split(o_t), split(both)).reshape(dw.shape)
        return 0

    lax.fori_loop(0, NCH, grad_step, 0)
    for h in range(H):
        db[:, :, :, h * DH:(h + 1) * DH] = (acc[h * DH:(h + 1) * DH] * scale).T.reshape(NZ, NY, la, DH)
    dq_y = start(sum_y(db, db1, 1))
    dw_y = start(sum_y(dw, dw1, 2))

    partner = (ctx, x * CORES + (1 - core))

    def first(i):
        return remote(dprob.at[0, rows(i)], one_recv.at[rows(i)], t1_s.at[i], t1_r.at[i], partner)

    def second(i, k):
        xp = other(x, k, NX)
        cols = pl.ds(pl.multiple_of(xp * blk, blk), blk)
        return remote(
            expo.at[0, rows(i), cols], x_recv.at[k - 1, rows(i)], tx_s.at[k, i], tx_r.at[k, i],
            (ctx, xp * CORES + core),
        )

    def forward(i):
        first(i).wait_recv()
        expo[0, rows(i)] += one_recv[rows(i)]
        for k in range(1, NX):
            second(i, k).start()

    def token_step(i, _):
        grads = split(kv[i])
        for xp in range(NX):
            b = pl.ds(pl.multiple_of((xp * CORES + (1 - core)) * blk, blk), blk)
            dprob[0, rows(i), xp * blk:(xp + 1) * blk] = dot3(grads, (wh[b], wl[b]), RHS_T)
        first(i).start()
        for xp in range(NX):
            b = pl.ds(pl.multiple_of((xp * CORES + core) * blk, blk), blk)
            expo[0, rows(i), xp * blk:(xp + 1) * blk] = dot3(grads, (wh[b], wl[b]), RHS_T)

        @pl.when(i > 0)
        def _():
            forward(i - 1)

        return 0

    quarter = NCH // 4
    lax.fori_loop(0, quarter, token_step, 0)
    wait(att_y)
    add_y(ab, ab1)
    att_z = start(sum_z(ab, ab2, 0))
    wait(dq_y)
    add_y(db, db1)
    dq_z = start(sum_z(db, db2, 1))

    lax.fori_loop(quarter, 2 * quarter, token_step, 0)
    wait(att_z)
    put(aall, add_z(ab, ab2))
    att_az = start(all_z(aall, 2))
    wait(dq_z)
    dq_mine = add_z(db, db2)
    put(dall, dq_mine)
    hbuf[0] = dq_mine
    dq_az = start(all_z(dall, 3))
    dq_h = start([
        remote(hbuf.at[0], hbuf.at[k], h_s.at[k], h_r.at[k], (ctx, other(head, k, NH))) for k in range(1, NH)
    ])

    lax.fori_loop(2 * quarter, 3 * quarter, token_step, 0)
    wait(att_az)
    att_ay = start(all_y(aall, 3))
    wait(dq_az)
    dq_ay = start(all_y(dall, 4))
    wait(wq_copies)
    wait(dq_h)
    mine_rows = pl.ds(pl.multiple_of(head * blk, blk), blk)
    lat_part = dot3(split(hbuf[0]), split(wq[mine_rows]), RHS_T)
    for k in range(1, NH):
        lat_part += dot3(split(hbuf[k]), split(wqr[k]), RHS_T)
    put(lall, lat_part)
    lat_az = start(all_z(lall, 4))
    wait(dw_y)
    add_y(dw, dw1)
    dw_z = start(sum_z(dw, dw2, 5))

    lax.fori_loop(3 * quarter, NCH, token_step, 0)
    forward(NCH - 1)
    wait(lat_az)
    lat_ay = start(all_y(lall, 5))
    wait(att_ay)
    att_t = aall[...].reshape(L, W).T
    dwo_o[...] = dot3(split(att_t), split(dout[...]))
    wait(dq_ay)
    dq_t = dall[...].reshape(L, W).T
    dwq_o[...] = dot3(split(dq_t), split(lat[...])).T
    wait(lat_ay)
    dlat_o[...] = lall[...].reshape(L, blk)

    def finish(i, _):
        cols = pl.ds(pl.multiple_of(x * blk, blk), blk)
        total = expo[0, rows(i), cols]
        for k in range(1, NX):
            second(i, k).wait_recv()
            total += x_recv[k - 1, rows(i)]
        dobs_o[rows(i)] = total
        first(i).wait_send()
        for k in range(1, NX):
            second(i, k).wait_send()
        return 0

    lax.fori_loop(0, NCH, finish, 0)
    wait(dw_z)
    dw_mine = add_z(dw, dw2)
    dwk_o[...] = dw_mine[:, :W]
    dwv_o[...] = dw_mine[:, W:]


def on_device(nc, nh, latents, observations, w_query, w_key, w_value, w_out, d_out):
    L, D = latents.shape
    T = observations.shape[0]
    W = w_query.shape[1]
    H, blk, la, r = W // DH, D // nh, L // nc, D // nc
    ny = 1 << ((nc.bit_length() - 1) // 2)
    nz, nx = nc // ny, nh // CORES
    tc = min(256, T // 4)
    nch = T // tc
    stat_rows = -(-3 * H // 8) * 8

    def vm(*shape, dtype=F32):
        return pltpu.VMEM(shape, dtype)

    def sems(*shape):
        return pltpu.SemaphoreType.DMA(shape)

    vmem = pl.BlockSpec(memory_space=pltpu.VMEM)
    out = lambda *s: jax.ShapeDtypeStruct(s, F32)
    return pl.pallas_call(
        functools.partial(kernel, (nc, nh, ny, tc)),
        out_shape=(out(L, blk), out(T, blk), out(D, W), out(r, W), out(r, W), out(W, D)),
        in_specs=[vmem, pl.BlockSpec(memory_space=pl.ANY)] + [vmem] * 5,
        out_specs=tuple([vmem] * 6),
        scratch_shapes=[
            vm(H, T, L), vm(H, T, L), vm(nch, tc, 2 * W), vm(2, tc, D),
            vm(D, 2 * W, dtype=BF16), vm(D, 2 * W, dtype=BF16),
            vm(H, L, 4 * DH, dtype=BF16), vm(H, L, 4 * DH, dtype=BF16),
            vm(H, L, 2 * DH, dtype=BF16), vm(H, L, 2 * DH, dtype=BF16),
            vm(stat_rows, L), vm(nc, stat_rows, L), vm(W, L),
            vm(T, nx * blk), vm(max(nx - 1, 1), T, blk),
            vm(nz, ny, r, 2 * W), vm(ny, nz, r, 2 * W), vm(nz, r, 2 * W),
            vm(nz, ny, la, W), vm(ny, nz, la, W), vm(nz, la, W),
            vm(nz, ny, la, W), vm(ny, nz, la, W), vm(nz, la, W),
            vm(nz, ny, la, W), vm(nz, ny, la, W), vm(nz, ny, la, blk),
            vm(nh, blk, W), vm(nh, la, W),
            sems(2), sems(nc), sems(nc), sems(nh), sems(nh), sems(nh), sems(nh),
            sems(nch), sems(nch), sems(nx, nch), sems(nx, nch),
            sems(6, ny), sems(6, ny), sems(6, nz), sems(6, nz),
        ],
        compiler_params=pltpu.CompilerParams(
            collective_id=0, has_side_effects=True, vmem_limit_bytes=63 * 2**20
        ),
        cost_estimate=pl.CostEstimate(flops=3 * 11 * 10**9, bytes_accessed=40 * 2**20, transcendentals=H * T * L),
    )(latents, observations, w_query, w_key, w_value, w_out, d_out)


def solution(mesh):
    placed = (
        P(),
        P("ctx", None),
        P(None, "head"),
        P(None, "head"),
        P(None, "head"),
        P("head", None),
        P(),
    )
    return jax.shard_map(
        functools.partial(on_device, mesh.shape["ctx"], mesh.shape["head"]),
        mesh=mesh,
        in_specs=placed,
        out_specs=(
            P(None, "head"),
            P("ctx", "head"),
            P(None, "head"),
            P("ctx", "head"),
            P("ctx", "head"),
            P("head", None),
        ),
        check_vma=False,
    )
```

profile of v0, /device:TPU:8, one launch (start us, length us, event | category | flops | bytes accessed | tf_op | source)
XLA Modules:
  0.0 110.9 jit_solution(3090368080904659564)
XLA Ops:
  0.6 102.0 %shard_map.118 = (f32[512,256]{1,0:T(8,128)}, f32[2048,256]{1,0:T(8,128)}, f32[1024,256]{1,0:T(8,128)}, f32[128,256]{1,0:T(8,128)}, f32[128,256]{1,0:T(8,128)}, /*index=5*/f32[256,1024]{1,0:T(8,128)}) custom-call(f32[512,1024]{1,0:T(8,128)} %lat.1, f32[2048,1024]{1,0:T(8,128)} %obs.1, f32[1024,256]{1,0:T(8,128)} %wq.1, f32[1024,256]{1,0:T(8,128)} %wk.1, ...), custom_call_target="tpu_custom_call" | custom-call | flops 32999999488 | bytes 41943040 | tf_op jit(solution)/shard_map/pallas_call | solution.py:396
  102.6 1.9 %copy.19 = f32[512,256]{1,0:T(8,128)} copy(f32[512,256]{1,0:T(8,128)} %get-tuple-element.12) | data formatting | bytes 1048576
  104.5 0.0 copy-start.1
  104.5 3.1 %copy.20 = f32[2048,256]{1,0:T(8,128)} copy(f32[2048,256]{1,0:T(8,128)} %get-tuple-element.13) | data formatting | bytes 4194304
  107.7 0.0 copy-done.1
  107.7 0.0 copy-start.3
  107.7 0.0 copy-start.2
  107.7 0.0 copy-start
  107.7 1.0 copy.21
  108.6 0.0 copy-done.3
  108.7 0.7 copy.22
  109.3 0.0 copy-done.2
  109.3 0.7 copy.23
  110.0 0.0 copy-done
  110.0 1.0 copy.24
Async XLA Ops:
  104.5 3.1 %copy-start.1 = (f32[1024,256]{1,0:T(8,128)S(1)}, f32[1024,256]{1,0:T(8,128)}, u32[]{:S(2)}) copy-start(f32[1024,256]{1,0:T(8,128)} %get-tuple-element.14) | copy-start | bytes 3145732
  107.7 1.0 copy-start.3
  107.7 1.7 %copy-start.2 = (f32[128,256]{1,0:T(8,128)S(1)}, f32[128,256]{1,0:T(8,128)}, u32[]{:S(2)}) copy-start(f32[128,256]{1,0:T(8,128)} %get-tuple-element.16) | copy-start | bytes 393220
  107.7 2.3 %copy-start = (f32[256,1024]{1,0:T(8,128)S(1)}, f32[256,1024]{1,0:T(8,128)}, u32[]{:S(2)}) copy-start(f32[256,1024]{1,0:T(8,128)} %get-tuple-element.17) | copy-start | bytes 3145732
where the time goes:
time: 111 us
  Pallas kernels  102 us (92%)
  local copies, waits for them, and re-layouts  8.28 us (7%)
    pallas_call x1, Pallas kernels, on_device(): pl.pallas_call(functools.partial(kernel, (nc, nh, ny, tc)), out_shape=(ou...  102 us
    unnamed x14, local copies, waits for them, and re-layouts  8.28 us

commit v1 on v0

--- a/solution.py
+++ b/solution.py
@@ -31,8 +31,7 @@
     return dot(ah, bh, dims) + (dot(ah, bl, dims) + dot(al, bh, dims))
 
 
-def wide_left(x):
-    hi, lo = split(x)
+def wide_left(hi, lo):
     return jnp.concatenate([hi, hi, lo, lo], axis=1)
 
 
@@ -47,28 +46,28 @@
     return both[:, :DH] + (both[:, DH:] + dot(lo, b_hi))
 
 
-def short_dot(a_t, b):
-    ah, al = split(a_t)
+def short_dot(hi, lo, b):
+    ah = hi.T
     bh, bl = split(b)
-    both = dot(jnp.concatenate([ah, al], axis=0), bh)
+    both = dot(jnp.concatenate([ah, lo.T], axis=0), bh)
     return both[:DH] + (both[DH:] + dot(ah, bl))
 
 
 def kernel(
     cfg,
     lat, obs, wq, wk, wv, wo, dout,
-    dlat_o, dobs_o, dwq_o, dwk_o, dwv_o, dwo_o,
-    expo, dprob, kv, obuf, wh, wl, q4, g4, qp, gp, stat, rstat, acc,
+    dlat_o, dobs_o, dq_o, dw_o, att_o,
+    expo, dprob, kvh, kvl, obuf, cbuf, wh, wl, q4, g4, qp, gp, stat, rstat, acc,
     one_recv, x_recv,
     dw, dw1, dw2, ab, ab1, ab2, db, db1, db2, aall, dall, lall, wqr, hbuf,
-    obs_sem, st_s, st_r, wq_s, wq_r, h_s, h_r, t1_s, t1_r, tx_s, tx_r,
-    y_s, y_r, z_s, z_r,
+    obs_sem, col_sem, st_s, st_r, wq_s, wq_r, h_s, h_r, t1_s, t1_r, tx_s, tx_r,
+    y_s, y_r, z_s, z_r, wy_s, wy_r, wz_s, wz_r, out_sem, res_sem,
 ):
     NC, NH, NY, TC = cfg
     NZ, NX = NC // NY, NH // CORES
     T, D = obs.shape
     L, W = lat.shape[0], wq.shape[1]
-    H, NCH, blk, la = W // DH, T // TC, D // NH, L // NC
+    H, NCH, blk, la, r = W // DH, T // TC, D // NH, L // NC, D // NC
     scale = 1.0 / math.sqrt(DH)
     ctx, head = lax.axis_index("ctx"), lax.axis_index("head")
     z, y = ctx // NY, lax.rem(ctx, NY)
@@ -127,17 +126,27 @@
         fetch(i).wait()
         o = split(obuf[lax.rem(i, 2)])
         both = dot3(o, (wh[...], wl[...]))
-        kv[i] = both
+        hi, lo = split(both)
+        kvh[i] = hi
+        kvl[i] = lo
         out = []
         for h in range(H):
-            s = dot(wide_left(both[:, h * DH:(h + 1) * DH]), q4[h], RHS_T)
+            k_h, v_h = slice(h * DH, (h + 1) * DH), slice(W + h * DH, W + (h + 1) * DH)
+            s = dot(wide_left(hi[:, k_h], lo[:, k_h]), q4[h], RHS_T)
             expo[h, rows(i)] = s
             out.append(jnp.maximum(tops[h], jnp.max(s, axis=0, keepdims=True)))
-            dprob[h, rows(i)] = dot(wide_left(both[:, W + h * DH:W + (h + 1) * DH]), g4[h], RHS_T)
+            dprob[h, rows(i)] = dot(wide_left(hi[:, v_h], lo[:, v_h]), g4[h], RHS_T)
         return tuple(out)
 
     tops = lax.fori_loop(0, NCH, scores_step, tuple(jnp.full((1, L), -3e38, F32) for _ in range(H)))
-    fetch(0).start()
+
+    def fetch_cols(j):
+        b = pl.multiple_of(other(z, 1 + j, NZ) * (NY * r), NY * r)
+        return pltpu.make_async_copy(obs.at[:, pl.ds(b, NY * r)], cbuf.at[j % 2], col_sem.at[j % 2])
+
+    fetch_cols(0).start()
+    if NZ > 1:
+        fetch_cols(1).start()
 
     def exp_step(i, sums):
         out = []
@@ -163,10 +172,9 @@
     acc[...] = jnp.zeros_like(acc)
 
     def acc_step(i, _):
-        both = kv[i]
         for h in range(H):
-            v_t = both[:, W + h * DH:W + (h + 1) * DH].T
-            acc[h * DH:(h + 1) * DH] += short_dot(v_t, expo[h, rows(i)])
+            v_h = slice(W + h * DH, W + (h + 1) * DH)
+            acc[h * DH:(h + 1) * DH] += short_dot(kvh[i, :, v_h], kvl[i, :, v_h], expo[h, rows(i)])
         return 0
 
     lax.fori_loop(0, NCH, acc_step, 0)
@@ -240,33 +248,6 @@
     att_y = start(sum_y(ab, ab1, 0))
 
     acc[...] = jnp.zeros_like(acc)
-    dw[...] = jnp.zeros_like(dw)
-
-    def grad_step(i, _):
-        @pl.when(i + 1 < NCH)
-        def _():
-            fetch(i + 1).start()
-
-        fetch(i).wait()
-        both = kv[i]
-        dk, dv = [], []
-        for h in range(H):
-            p = expo[h, rows(i)] * weights[h]
-            ds = p * (dprob[h, rows(i)] - deltas[h])
-            dk.append(narrow_dot(ds, qp[h], qp[h, :, :DH]))
-            dv.append(narrow_dot(p, gp[h], gp[h, :, :DH]))
-            acc[h * DH:(h + 1) * DH] += short_dot(both[:, h * DH:(h + 1) * DH].T, ds)
-        both = jnp.concatenate(dk + dv, axis=1)
-        kv[i] = both
-        o_t = obuf[lax.rem(i, 2)].T
-        dw[...] += dot3(split(o_t), split(both)).reshape(dw.shape)
-        return 0
-
-    lax.fori_loop(0, NCH, grad_step, 0)
-    for h in range(H):
-        db[:, :, :, h * DH:(h + 1) * DH] = (acc[h * DH:(h + 1) * DH] * scale).T.reshape(NZ, NY, la, DH)
-    dq_y = start(sum_y(db, db1, 1))
-    dw_y = start(sum_y(dw, dw1, 2))
 
     partner = (ctx, x * CORES + (1 - core))
 
@@ -287,8 +268,17 @@
         for k in range(1, NX):
             second(i, k).start()
 
-    def token_step(i, _):
-        grads = split(kv[i])
+    def grad_step(i, _):
+        dk, dv = [], []
+        for h in range(H):
+            k_h = slice(h * DH, (h + 1) * DH)
+            p = expo[h, rows(i)] * weights[h]
+            ds = p * (dprob[h, rows(i)] - deltas[h])
+            dk.append(narrow_dot(ds, qp[h], qp[h, :, :DH]))
+            dv.append(narrow_dot(p, gp[h], gp[h, :, :DH]))
+            acc[h * DH:(h + 1) * DH] += short_dot(kvh[i, :, k_h], kvl[i, :, k_h], ds)
+        grads = split(jnp.concatenate(dk + dv, axis=1))
+        kvh[i], kvl[i] = grads
         for xp in range(NX):
             b = pl.ds(pl.multiple_of((xp * CORES + (1 - core)) * blk, blk), blk)
             dprob[0, rows(i), xp * blk:(xp + 1) * blk] = dot3(grads, (wh[b], wl[b]), RHS_T)
@@ -304,56 +294,110 @@
         return 0
 
     quarter = NCH // 4
-    lax.fori_loop(0, quarter, token_step, 0)
+    lax.fori_loop(0, quarter, grad_step, 0)
     wait(att_y)
     add_y(ab, ab1)
     att_z = start(sum_z(ab, ab2, 0))
-    wait(dq_y)
-    add_y(db, db1)
-    dq_z = start(sum_z(db, db2, 1))
-
-    lax.fori_loop(quarter, 2 * quarter, token_step, 0)
+    lax.fori_loop(quarter, 2 * quarter, grad_step, 0)
     wait(att_z)
     put(aall, add_z(ab, ab2))
     att_az = start(all_z(aall, 2))
-    wait(dq_z)
-    dq_mine = add_z(db, db2)
-    put(dall, dq_mine)
-    hbuf[0] = dq_mine
-    dq_az = start(all_z(dall, 3))
-    dq_h = start([
-        remote(hbuf.at[0], hbuf.at[k], h_s.at[k], h_r.at[k], (ctx, other(head, k, NH))) for k in range(1, NH)
-    ])
-
-    lax.fori_loop(2 * quarter, 3 * quarter, token_step, 0)
+    lax.fori_loop(2 * quarter, 3 * quarter, grad_step, 0)
     wait(att_az)
     att_ay = start(all_y(aall, 3))
-    wait(dq_az)
-    dq_ay = start(all_y(dall, 4))
-    wait(wq_copies)
-    wait(dq_h)
-    mine_rows = pl.ds(pl.multiple_of(head * blk, blk), blk)
-    lat_part = dot3(split(hbuf[0]), split(wq[mine_rows]), RHS_T)
-    for k in range(1, NH):
-        lat_part += dot3(split(hbuf[k]), split(wqr[k]), RHS_T)
-    put(lall, lat_part)
-    lat_az = start(all_z(lall, 4))
-    wait(dw_y)
-    add_y(dw, dw1)
-    dw_z = start(sum_z(dw, dw2, 5))
-
-    lax.fori_loop(3 * quarter, NCH, token_step, 0)
-    forward(NCH - 1)
-    wait(lat_az)
+    lax.fori_loop(3 * quarter, NCH, grad_step, 0)
+    for h in range(H):
+        db[:, :, :, h * DH:(h + 1) * DH] = (acc[h * DH:(h + 1) * DH] * scale).T.reshape(NZ, NY, la, DH)
+    pending = {"y": start(sum_y(db, db1, 1))}
+
+    def dq_to_z():
+        wait(pending["y"])
+        add_y(db, db1)
+        pending["z"] = start(sum_z(db, db2, 1))
+
+    def dq_to_all():
+        wait(pending["z"])
+        mine = add_z(db, db2)
+        put(dall, mine)
+        hbuf[0] = mine
+        pending["az"] = start(all_z(dall, 3))
+        pending["h"] = start([
+            remote(hbuf.at[0], hbuf.at[k], h_s.at[k], h_r.at[k], (ctx, other(head, k, NH))) for k in range(1, NH)
+        ])
+
+    def latents_part():
+        wait(pending["az"])
+        pending["ay"] = start(all_y(dall, 4))
+        wait(wq_copies)
+        wait(pending["h"])
+        mine_rows = pl.ds(pl.multiple_of(head * blk, blk), blk)
+        lat_part = dot3(split(hbuf[0]), split(wq[mine_rows]), RHS_T)
+        for k in range(1, NH):
+            lat_part += dot3(split(hbuf[k]), split(wqr[k]), RHS_T)
+        put(lall, lat_part)
+        pending["lat"] = start(all_z(lall, 4))
+
+    stages = [dq_to_z, dq_to_all, latents_part]
+
+    def w_y(j):
+        b = other(z, 1 + j, NZ)
+        return [
+            remote(
+                dw.at[b, other(y, k, NY)], dw1.at[k, j], wy_s.at[k, j], wy_r.at[k, j],
+                (z * NY + other(y, k, NY), head),
+            )
+            for k in range(1, NY)
+        ]
+
+    def w_z(j):
+        b = other(z, 1 + j, NZ)
+        return remote(dw.at[b, y], dw2.at[1 + j], wz_s.at[1 + j], wz_r.at[1 + j], (b * NY + y, head))
+
+    def w_sum(j):
+        wait(w_y(j))
+        b = pl.ds(other(z, 1 + j, NZ), 1)
+        total = dw[b, pl.ds(y, 1)]
+        for k in range(1, NY):
+            total += dw1[k, j].reshape(total.shape)
+        dw[b, pl.ds(y, 1)] = total
+        if j < NZ - 1:
+            w_z(j).start()
+
+    for j in range(NZ):
+        fetch_cols(j).wait()
+        zb = pl.ds(other(z, 1 + j, NZ), 1)
+        dw[zb] = jnp.zeros((1, NY, r, 2 * W), F32)
+
+        def w_step(i, _, j=j, zb=zb):
+            o_t = cbuf[j % 2, rows(i)].T
+            dw[zb] += dot3(split(o_t), (kvh[i], kvl[i])).reshape(1, NY, r, 2 * W)
+            return 0
+
+        lax.fori_loop(0, NCH, w_step, 0)
+        if j + 2 < NZ:
+            fetch_cols(j + 2).start()
+        start(w_y(j))
+        if j == 0:
+            forward(NCH - 1)
+        else:
+            w_sum(j - 1)
+            if stages:
+                stages.pop(0)()
+    for stage in stages:
+        stage()
+    wait(att_ay)
+    results = start([pltpu.make_async_copy(aall, att_o, res_sem.at[0])])
+    wait(pending["lat"])
     lat_ay = start(all_y(lall, 5))
-    wait(att_ay)
-    att_t = aall[...].reshape(L, W).T
-    dwo_o[...] = dot3(split(att_t), split(dout[...]))
-    wait(dq_ay)
-    dq_t = dall[...].reshape(L, W).T
-    dwq_o[...] = dot3(split(dq_t), split(lat[...])).T
+    wait(pending["ay"])
+    results += start([pltpu.make_async_copy(dall, dq_o, res_sem.at[1])])
+    w_sum(NZ - 1)
     wait(lat_ay)
-    dlat_o[...] = lall[...].reshape(L, blk)
+    results += start([pltpu.make_async_copy(lall, dlat_o, res_sem.at[2])])
+
+    def out_copy(i):
+        cols = pl.ds(pl.multiple_of(x * blk, blk), blk)
+        return pltpu.make_async_copy(expo.at[0, rows(i), cols], dobs_o.at[rows(i)], out_sem.at[i])
 
     def finish(i, _):
         cols = pl.ds(pl.multiple_of(x * blk, blk), blk)
@@ -361,17 +405,50 @@
         for k in range(1, NX):
             second(i, k).wait_recv()
             total += x_recv[k - 1, rows(i)]
-        dobs_o[rows(i)] = total
+        expo[0, rows(i), cols] = total
+        out_copy(i).start()
         first(i).wait_send()
         for k in range(1, NX):
             second(i, k).wait_send()
         return 0
 
     lax.fori_loop(0, NCH, finish, 0)
-    wait(dw_z)
-    dw_mine = add_z(dw, dw2)
-    dwk_o[...] = dw_mine[:, :W]
-    dwv_o[...] = dw_mine[:, W:]
+    dw_mine = dw[pl.ds(z, 1), pl.ds(y, 1)].reshape(r, 2 * W)
+    for j in range(NZ - 1):
+        w_z(j).wait()
+        dw_mine += dw2[1 + j]
+    dw2[0] = dw_mine
+    results += start([pltpu.make_async_copy(dw2.at[0], dw_o, res_sem.at[3])])
+
+    def drain(i, _):
+        out_copy(i).wait()
+        return 0
+
+    lax.fori_loop(0, NCH, drain, 0)
+    wait(results)
+
+
+def last_kernel(att, dq, lat, dout, dlat, dobs, dw, dlat_o, dobs_o, dwq_o, dwk_o, dwv_o, dwo_o, sem):
+    W = dq.shape[1]
+    moves = [
+        pltpu.make_async_copy(dobs, dobs_o, sem.at[0]),
+        pltpu.make_async_copy(dlat, dlat_o, sem.at[1]),
+        pltpu.make_async_copy(dw.at[:, pl.ds(0, W)], dwk_o, sem.at[2]),
+        pltpu.make_async_copy(dw.at[:, pl.ds(W, W)], dwv_o, sem.at[3]),
+    ]
+
+    @pl.when(pl.program_id(0) == 0)
+    def _():
+        for c in moves:
+            c.start()
+
+    dwo_o[...] = dot3(split(att[...].T), split(dout[...]))
+    dwq_o[...] = dot3(split(lat[...].T), split(dq[...]))
+
+    @pl.when(pl.program_id(0) == pl.num_programs(0) - 1)
+    def _():
+        for c in moves:
+            c.wait()
 
 
 def on_device(nc, nh, latents, observations, w_query, w_key, w_value, w_out, d_out):
@@ -393,13 +470,15 @@
 
     vmem = pl.BlockSpec(memory_space=pltpu.VMEM)
     out = lambda *s: jax.ShapeDtypeStruct(s, F32)
-    return pl.pallas_call(
+    anywhere = pl.BlockSpec(memory_space=pl.ANY)
+    dlat, dobs, dq, dw, att = pl.pallas_call(
         functools.partial(kernel, (nc, nh, ny, tc)),
-        out_shape=(out(L, blk), out(T, blk), out(D, W), out(r, W), out(r, W), out(W, D)),
-        in_specs=[vmem, pl.BlockSpec(memory_space=pl.ANY)] + [vmem] * 5,
-        out_specs=tuple([vmem] * 6),
+        out_shape=(out(nz, ny, la, blk), out(T, blk), out(nz, ny, la, W), out(r, 2 * W), out(nz, ny, la, W)),
+        in_specs=[vmem, anywhere] + [vmem] * 5,
+        out_specs=(anywhere,) * 5,
         scratch_shapes=[
-            vm(H, T, L), vm(H, T, L), vm(nch, tc, 2 * W), vm(2, tc, D),
+            vm(H, T, L), vm(H, T, L), vm(nch, tc, 2 * W, dtype=BF16), vm(nch, tc, 2 * W, dtype=BF16),
+            vm(2, tc, D), vm(2, T, ny * r),
             vm(D, 2 * W, dtype=BF16), vm(D, 2 * W, dtype=BF16),
             vm(H, L, 4 * DH, dtype=BF16), vm(H, L, 4 * DH, dtype=BF16),
             vm(H, L, 2 * DH, dtype=BF16), vm(H, L, 2 * DH, dtype=BF16),
@@ -410,15 +489,32 @@
             vm(nz, ny, la, W), vm(ny, nz, la, W), vm(nz, la, W),
             vm(nz, ny, la, W), vm(nz, ny, la, W), vm(nz, ny, la, blk),
             vm(nh, blk, W), vm(nh, la, W),
-            sems(2), sems(nc), sems(nc), sems(nh), sems(nh), sems(nh), sems(nh),
+            sems(2), sems(2), sems(nc), sems(nc), sems(nh), sems(nh), sems(nh), sems(nh),
             sems(nch), sems(nch), sems(nx, nch), sems(nx, nch),
             sems(6, ny), sems(6, ny), sems(6, nz), sems(6, nz),
+            sems(ny, nz), sems(ny, nz), sems(nz), sems(nz), sems(nch), sems(4),
         ],
         compiler_params=pltpu.CompilerParams(
             collective_id=0, has_side_effects=True, vmem_limit_bytes=63 * 2**20
         ),
         cost_estimate=pl.CostEstimate(flops=3 * 11 * 10**9, bytes_accessed=40 * 2**20, transcendentals=H * T * L),
     )(latents, observations, w_query, w_key, w_value, w_out, d_out)
+    wide = D // 4
+    whole = pl.BlockSpec((L, W), lambda i: (0, 0))
+    columns = pl.BlockSpec((L, wide), lambda i: (0, i))
+    return pl.pallas_call(
+        last_kernel,
+        grid=(4,),
+        out_shape=(out(L, blk), out(T, blk), out(D, W), out(r, W), out(r, W), out(W, D)),
+        in_specs=[whole, whole, columns, columns, anywhere, anywhere, anywhere],
+        out_specs=(
+            anywhere, anywhere, pl.BlockSpec((wide, W), lambda i: (i, 0)),
+            anywhere, anywhere, pl.BlockSpec((W, wide), lambda i: (0, i)),
+        ),
+        scratch_shapes=[sems(4)],
+        compiler_params=pltpu.CompilerParams(vmem_limit_bytes=62 * 2**20),
+        cost_estimate=pl.CostEstimate(flops=12 * L * D * W, bytes_accessed=20 * 2**20, transcendentals=0),
+    )(att.reshape(L, W), dq.reshape(L, W), latents, d_out, dlat.reshape(L, blk), dobs, dw)
 
 
 def solution(mesh):

time: 111 us -> 209 us (1.88); the launches traced: 111 us -> 207 us
  Pallas kernels: 102 us -> 206 us
  local copies, waits for them, and re-layouts: 8.28 us -> 0 us
    pallas_call x0 -> x1, Pallas kernels: none -> 91 us  [on_device(): pl.pallas_call(last_kernel, grid=(4,), out_shape=(out(L, blk), out(T, blk...]
    pallas_call x1, Pallas kernels: 102 us -> 115 us  [on_device(): pl.pallas_call(functools.partial(kernel, (nc, nh, ny, tc)), out_shape=(ou...]
    unnamed x14 -> x0, local copies, waits for them, and re-layouts: 8.28 us -> none
where the time goes in v1:
time: 209 us; the launch traced here: 207 us
  Pallas kernels  206 us (99%)
    pallas_call x1, Pallas kernels, on_device(): pl.pallas_call(functools.partial(kernel, (nc, nh, ny, tc)), out_shape=(ou...  115 us
    pallas_call x1, Pallas kernels, on_device(): pl.pallas_call(last_kernel, grid=(4,), out_shape=(out(L, blk), out(T, blk...  91 us

profile of v1, /device:TPU:8, one launch (start us, length us, event | category | flops | bytes accessed | tf_op | source)
XLA Modules:
  0.0 206.6 jit_solution(13938379501080509046)
XLA Ops:
  0.6 115.0 %shard_map.118 = (f32[4,2,64,256]{3,2,1,0:T(8,128)}, f32[2048,256]{1,0:T(8,128)}, f32[4,2,64,256]{3,2,1,0:T(8,128)}, f32[128,512]{1,0:T(8,128)}, f32[4,2,64,256]{3,2,1,0:T(8,128)}) custom-call(f32[512,1024]{1,0:T(8,128)} %lat.3, f32[2048,1024]{1,0:T(8,128)} %obs.1, f32[1024,256]{1,0:T(8,128)} %wq.1, f32[1024,256]{1,0:T(8,128)} %wk.1, f32[1024,256]{1,0:T(8,128)} %wv.1, ...), custom_call_target="tpu_custom_call" | custom-call | flops 32999999488 | bytes 41943040 | tf_op jit(solution)/shard_map/pallas_call | solution.py:474
  115.6 91.0 %shard_map.119 = (f32[512,256]{1,0:T(8,128)}, f32[2048,256]{1,0:T(8,128)}, f32[1024,256]{1,0:T(8,128)}, f32[128,256]{1,0:T(8,128)}, f32[128,256]{1,0:T(8,128)}, /*index=5*/f32[256,1024]{1,0:T(8,128)}) custom-call(f32[512,256]{1,0:T(8,128)} %bitcast.5, f32[512,256]{1,0:T(8,128)} %bitcast.4, f32[512,1024]{1,0:T(8,128)} %lat.3, f32[512,1024]{1,0:T(8,128)} %dout.3, ...), custom_call_target="tpu_custom_call" | custom-call | flops 1610612736 | bytes 20971520 | tf_op jit(solution)/shard_map/pallas_call | solution.py:505

commit v2 on v1

--- a/solution.py
+++ b/solution.py
@@ -31,7 +31,8 @@
     return dot(ah, bh, dims) + (dot(ah, bl, dims) + dot(al, bh, dims))
 
 
-def wide_left(hi, lo):
+def wide_left(x):
+    hi, lo = split(x)
     return jnp.concatenate([hi, hi, lo, lo], axis=1)
 
 
@@ -46,10 +47,10 @@
     return both[:, :DH] + (both[:, DH:] + dot(lo, b_hi))
 
 
-def short_dot(hi, lo, b):
-    ah = hi.T
+def short_dot(a_t, b):
+    ah, al = split(a_t)
     bh, bl = split(b)
-    both = dot(jnp.concatenate([ah, lo.T], axis=0), bh)
+    both = dot(jnp.concatenate([ah, al], axis=0), bh)
     return both[:DH] + (both[DH:] + dot(ah, bl))
 
 
@@ -57,10 +58,10 @@
     cfg,
     lat, obs, wq, wk, wv, wo, dout,
     dlat_o, dobs_o, dq_o, dw_o, att_o,
-    expo, dprob, kvh, kvl, obuf, cbuf, wh, wl, q4, g4, qp, gp, stat, rstat, acc,
+    expo, dprob, kv, obuf, wh, wl, q4, g4, qp, gp, stat, rstat, acc,
     one_recv, x_recv,
     dw, dw1, dw2, ab, ab1, ab2, db, db1, db2, aall, dall, lall, wqr, hbuf,
-    obs_sem, col_sem, st_s, st_r, wq_s, wq_r, h_s, h_r, t1_s, t1_r, tx_s, tx_r,
+    obs_sem, st_s, st_r, wq_s, wq_r, h_s, h_r, t1_s, t1_r, tx_s, tx_r,
     y_s, y_r, z_s, z_r, wy_s, wy_r, wz_s, wz_r, out_sem, res_sem,
 ):
     NC, NH, NY, TC = cfg
@@ -126,27 +127,17 @@
         fetch(i).wait()
         o = split(obuf[lax.rem(i, 2)])
         both = dot3(o, (wh[...], wl[...]))
-        hi, lo = split(both)
-        kvh[i] = hi
-        kvl[i] = lo
+        kv[i] = both
         out = []
         for h in range(H):
-            k_h, v_h = slice(h * DH, (h + 1) * DH), slice(W + h * DH, W + (h + 1) * DH)
-            s = dot(wide_left(hi[:, k_h], lo[:, k_h]), q4[h], RHS_T)
+            s = dot(wide_left(both[:, h * DH:(h + 1) * DH]), q4[h], RHS_T)
             expo[h, rows(i)] = s
             out.append(jnp.maximum(tops[h], jnp.max(s, axis=0, keepdims=True)))
-            dprob[h, rows(i)] = dot(wide_left(hi[:, v_h], lo[:, v_h]), g4[h], RHS_T)
+            dprob[h, rows(i)] = dot(wide_left(both[:, W + h * DH:W + (h + 1) * DH]), g4[h], RHS_T)
         return tuple(out)
 
     tops = lax.fori_loop(0, NCH, scores_step, tuple(jnp.full((1, L), -3e38, F32) for _ in range(H)))
-
-    def fetch_cols(j):
-        b = pl.multiple_of(other(z, 1 + j, NZ) * (NY * r), NY * r)
-        return pltpu.make_async_copy(obs.at[:, pl.ds(b, NY * r)], cbuf.at[j % 2], col_sem.at[j % 2])
-
-    fetch_cols(0).start()
-    if NZ > 1:
-        fetch_cols(1).start()
+    fetch(0).start()
 
     def exp_step(i, sums):
         out = []
@@ -172,9 +163,10 @@
     acc[...] = jnp.zeros_like(acc)
 
     def acc_step(i, _):
+        both = kv[i]
         for h in range(H):
-            v_h = slice(W + h * DH, W + (h + 1) * DH)
-            acc[h * DH:(h + 1) * DH] += short_dot(kvh[i, :, v_h], kvl[i, :, v_h], expo[h, rows(i)])
+            v_t = both[:, W + h * DH:W + (h + 1) * DH].T
+            acc[h * DH:(h + 1) * DH] += short_dot(v_t, expo[h, rows(i)])
         return 0
 
     lax.fori_loop(0, NCH, acc_step, 0)
@@ -248,6 +240,7 @@
     att_y = start(sum_y(ab, ab1, 0))
 
     acc[...] = jnp.zeros_like(acc)
+    dw[...] = jnp.zeros_like(dw)
 
     partner = (ctx, x * CORES + (1 - core))
 
@@ -268,17 +261,8 @@
         for k in range(1, NX):
             second(i, k).start()
 
-    def grad_step(i, _):
-        dk, dv = [], []
-        for h in range(H):
-            k_h = slice(h * DH, (h + 1) * DH)
-            p = expo[h, rows(i)] * weights[h]
-            ds = p * (dprob[h, rows(i)] - deltas[h])
-            dk.append(narrow_dot(ds, qp[h], qp[h, :, :DH]))
-            dv.append(narrow_dot(p, gp[h], gp[h, :, :DH]))
-            acc[h * DH:(h + 1) * DH] += short_dot(kvh[i, :, k_h], kvl[i, :, k_h], ds)
-        grads = split(jnp.concatenate(dk + dv, axis=1))
-        kvh[i], kvl[i] = grads
+    def token_step(i, _):
+        grads = split(kv[i])
         for xp in range(NX):
             b = pl.ds(pl.multiple_of((xp * CORES + (1 - core)) * blk, blk), blk)
             dprob[0, rows(i), xp * blk:(xp + 1) * blk] = dot3(grads, (wh[b], wl[b]), RHS_T)
@@ -287,25 +271,76 @@
             b = pl.ds(pl.multiple_of((xp * CORES + core) * blk, blk), blk)
             expo[0, rows(i), xp * blk:(xp + 1) * blk] = dot3(grads, (wh[b], wl[b]), RHS_T)
 
-        @pl.when(i > 0)
+        @pl.when((i > 0) & (i != NCH // 2))
         def _():
             forward(i - 1)
 
         return 0
 
+    def grad_step(i, _):
+        @pl.when(i + 1 < NCH)
+        def _():
+            fetch(i + 1).start()
+
+        fetch(i).wait()
+        both = kv[i]
+        dk, dv = [], []
+        for h in range(H):
+            p = expo[h, rows(i)] * weights[h]
+            ds = p * (dprob[h, rows(i)] - deltas[h])
+            dk.append(narrow_dot(ds, qp[h], qp[h, :, :DH]))
+            dv.append(narrow_dot(p, gp[h], gp[h, :, :DH]))
+            acc[h * DH:(h + 1) * DH] += short_dot(both[:, h * DH:(h + 1) * DH].T, ds)
+        both = jnp.concatenate(dk + dv, axis=1)
+        kv[i] = both
+        o_t = obuf[lax.rem(i, 2)].T
+        dw[...] += dot3(split(o_t), split(both)).reshape(dw.shape)
+        return 0
+
+    def both_step(i, _):
+        grad_step(i, 0)
+        token_step(i, 0)
+        return 0
+
     quarter = NCH // 4
-    lax.fori_loop(0, quarter, grad_step, 0)
+    lax.fori_loop(0, quarter, both_step, 0)
     wait(att_y)
     add_y(ab, ab1)
     att_z = start(sum_z(ab, ab2, 0))
-    lax.fori_loop(quarter, 2 * quarter, grad_step, 0)
+    lax.fori_loop(quarter, 2 * quarter, both_step, 0)
     wait(att_z)
     put(aall, add_z(ab, ab2))
     att_az = start(all_z(aall, 2))
     lax.fori_loop(2 * quarter, 3 * quarter, grad_step, 0)
+    forward(2 * quarter - 1)
     wait(att_az)
     att_ay = start(all_y(aall, 3))
     lax.fori_loop(3 * quarter, NCH, grad_step, 0)
+
+    def w_y(j):
+        b = other(z, 1 + j, NZ)
+        return [
+            remote(
+                dw.at[b, other(y, k, NY)], dw1.at[k, j], wy_s.at[k, j], wy_r.at[k, j],
+                (z * NY + other(y, k, NY), head),
+            )
+            for k in range(1, NY)
+        ]
+
+    def w_z(j):
+        b = other(z, 1 + j, NZ)
+        return remote(dw.at[b, y], dw2.at[1 + j], wz_s.at[1 + j], wz_r.at[1 + j], (b * NY + y, head))
+
+    def w_sum(j):
+        wait(w_y(j))
+        b = pl.ds(other(z, 1 + j, NZ), 1)
+        total = dw[b, pl.ds(y, 1)]
+        for k in range(1, NY):
+            total += dw1[k, j].reshape(total.shape)
+        dw[b, pl.ds(y, 1)] = total
+        if j < NZ - 1:
+            w_z(j).start()
+
     for h in range(H):
         db[:, :, :, h * DH:(h + 1) * DH] = (acc[h * DH:(h + 1) * DH] * scale).T.reshape(NZ, NY, la, DH)
     pending = {"y": start(sum_y(db, db1, 1))}
@@ -339,61 +374,27 @@
 
     stages = [dq_to_z, dq_to_all, latents_part]
 
-    def w_y(j):
-        b = other(z, 1 + j, NZ)
-        return [
-            remote(
-                dw.at[b, other(y, k, NY)], dw1.at[k, j], wy_s.at[k, j], wy_r.at[k, j],
-                (z * NY + other(y, k, NY), head),
-            )
-            for k in range(1, NY)
-        ]
-
-    def w_z(j):
-        b = other(z, 1 + j, NZ)
-        return remote(dw.at[b, y], dw2.at[1 + j], wz_s.at[1 + j], wz_r.at[1 + j], (b * NY + y, head))
-
-    def w_sum(j):
-        wait(w_y(j))
-        b = pl.ds(other(z, 1 + j, NZ), 1)
-        total = dw[b, pl.ds(y, 1)]
-        for k in range(1, NY):
-            total += dw1[k, j].reshape(total.shape)
-        dw[b, pl.ds(y, 1)] = total
-        if j < NZ - 1:
-            w_z(j).start()
-
     for j in range(NZ):
-        fetch_cols(j).wait()
-        zb = pl.ds(other(z, 1 + j, NZ), 1)
-        dw[zb] = jnp.zeros((1, NY, r, 2 * W), F32)
-
-        def w_step(i, _, j=j, zb=zb):
-            o_t = cbuf[j % 2, rows(i)].T
-            dw[zb] += dot3(split(o_t), (kvh[i], kvl[i])).reshape(1, NY, r, 2 * W)
-            return 0
-
-        lax.fori_loop(0, NCH, w_step, 0)
-        if j + 2 < NZ:
-            fetch_cols(j + 2).start()
         start(w_y(j))
-        if j == 0:
-            forward(NCH - 1)
-        else:
-            w_sum(j - 1)
-            if stages:
-                stages.pop(0)()
-    for stage in stages:
-        stage()
+
+    todo = [functools.partial(w_sum, j) for j in range(NZ - 1)]
+    lax.fori_loop(2 * quarter, 3 * quarter, token_step, 0)
+    stages.pop(0)()
+    todo.pop(0)()
+    lax.fori_loop(3 * quarter, NCH, token_step, 0)
+    forward(NCH - 1)
+    while stages or todo:
+        if stages:
+            stages.pop(0)()
+        if todo:
+            todo.pop(0)()
     wait(att_ay)
     results = start([pltpu.make_async_copy(aall, att_o, res_sem.at[0])])
     wait(pending["lat"])
     lat_ay = start(all_y(lall, 5))
+    w_sum(NZ - 1)
     wait(pending["ay"])
     results += start([pltpu.make_async_copy(dall, dq_o, res_sem.at[1])])
-    w_sum(NZ - 1)
-    wait(lat_ay)
-    results += start([pltpu.make_async_copy(lall, dlat_o, res_sem.at[2])])
 
     def out_copy(i):
         cols = pl.ds(pl.multiple_of(x * blk, blk), blk)
@@ -413,6 +414,8 @@
         return 0
 
     lax.fori_loop(0, NCH, finish, 0)
+    wait(lat_ay)
+    results += start([pltpu.make_async_copy(lall, dlat_o, res_sem.at[2])])
     dw_mine = dw[pl.ds(z, 1), pl.ds(y, 1)].reshape(r, 2 * W)
     for j in range(NZ - 1):
         w_z(j).wait()
@@ -428,27 +431,14 @@
     wait(results)
 
 
-def last_kernel(att, dq, lat, dout, dlat, dobs, dw, dlat_o, dobs_o, dwq_o, dwk_o, dwv_o, dwo_o, sem):
+def last_kernel(att, dq, lat, dout, dlat, dobs, dw, dlat_o, dobs_o, dwq_o, dwk_o, dwv_o, dwo_o):
     W = dq.shape[1]
-    moves = [
-        pltpu.make_async_copy(dobs, dobs_o, sem.at[0]),
-        pltpu.make_async_copy(dlat, dlat_o, sem.at[1]),
-        pltpu.make_async_copy(dw.at[:, pl.ds(0, W)], dwk_o, sem.at[2]),
-        pltpu.make_async_copy(dw.at[:, pl.ds(W, W)], dwv_o, sem.at[3]),
-    ]
-
-    @pl.when(pl.program_id(0) == 0)
-    def _():
-        for c in moves:
-            c.start()
-
     dwo_o[...] = dot3(split(att[...].T), split(dout[...]))
     dwq_o[...] = dot3(split(lat[...].T), split(dq[...]))
-
-    @pl.when(pl.program_id(0) == pl.num_programs(0) - 1)
-    def _():
-        for c in moves:
-            c.wait()
+    dobs_o[...] = dobs[...]
+    dlat_o[...] = dlat[...]
+    dwk_o[...] = dw[:, :W]
+    dwv_o[...] = dw[:, W:]
 
 
 def on_device(nc, nh, latents, observations, w_query, w_key, w_value, w_out, d_out):
@@ -477,8 +467,7 @@
         in_specs=[vmem, anywhere] + [vmem] * 5,
         out_specs=(anywhere,) * 5,
         scratch_shapes=[
-            vm(H, T, L), vm(H, T, L), vm(nch, tc, 2 * W, dtype=BF16), vm(nch, tc, 2 * W, dtype=BF16),
-            vm(2, tc, D), vm(2, T, ny * r),
+            vm(H, T, L), vm(H, T, L), vm(nch, tc, 2 * W), vm(2, tc, D),
             vm(D, 2 * W, dtype=BF16), vm(D, 2 * W, dtype=BF16),
             vm(H, L, 4 * DH, dtype=BF16), vm(H, L, 4 * DH, dtype=BF16),
             vm(H, L, 2 * DH, dtype=BF16), vm(H, L, 2 * DH, dtype=BF16),
@@ -489,7 +478,7 @@
             vm(nz, ny, la, W), vm(ny, nz, la, W), vm(nz, la, W),
             vm(nz, ny, la, W), vm(nz, ny, la, W), vm(nz, ny, la, blk),
             vm(nh, blk, W), vm(nh, la, W),
-            sems(2), sems(2), sems(nc), sems(nc), sems(nh), sems(nh), sems(nh), sems(nh),
+            sems(2), sems(nc), sems(nc), sems(nh), sems(nh), sems(nh), sems(nh),
             sems(nch), sems(nch), sems(nx, nch), sems(nx, nch),
             sems(6, ny), sems(6, ny), sems(6, nz), sems(6, nz),
             sems(ny, nz), sems(ny, nz), sems(nz), sems(nz), sems(nch), sems(4),
@@ -499,19 +488,28 @@
         ),
         cost_estimate=pl.CostEstimate(flops=3 * 11 * 10**9, bytes_accessed=40 * 2**20, transcendentals=H * T * L),
     )(latents, observations, w_query, w_key, w_value, w_out, d_out)
-    wide = D // 4
-    whole = pl.BlockSpec((L, W), lambda i: (0, 0))
+    steps = 4
+    wide = D // steps
+
+    def whole(*shape):
+        return pl.BlockSpec(shape, lambda i: (0, 0))
+
+    def by_rows(rows, columns):
+        return pl.BlockSpec((rows, columns), lambda i: (i, 0))
+
     columns = pl.BlockSpec((L, wide), lambda i: (0, i))
     return pl.pallas_call(
         last_kernel,
-        grid=(4,),
+        grid=(steps,),
         out_shape=(out(L, blk), out(T, blk), out(D, W), out(r, W), out(r, W), out(W, D)),
-        in_specs=[whole, whole, columns, columns, anywhere, anywhere, anywhere],
+        in_specs=[
+            whole(L, W), whole(L, W), columns, columns,
+            by_rows(L // steps, blk), by_rows(T // steps, blk), by_rows(r // steps, 2 * W),
+        ],
         out_specs=(
-            anywhere, anywhere, pl.BlockSpec((wide, W), lambda i: (i, 0)),
-            anywhere, anywhere, pl.BlockSpec((W, wide), lambda i: (0, i)),
+            by_rows(L // steps, blk), by_rows(T // steps, blk), by_rows(wide, W),
+            by_rows(r // steps, W), by_rows(r // steps, W), pl.BlockSpec((W, wide), lambda i: (0, i)),
         ),
-        scratch_shapes=[sems(4)],
         compiler_params=pltpu.CompilerParams(vmem_limit_bytes=62 * 2**20),
         cost_estimate=pl.CostEstimate(flops=12 * L * D * W, bytes_accessed=20 * 2**20, transcendentals=0),
     )(att.reshape(L, W), dq.reshape(L, W), latents, d_out, dlat.reshape(L, blk), dobs, dw)

time: 209 us -> 117 us (0.56)
  Pallas kernels: 206 us -> 115 us
    pallas_call x1, Pallas kernels: 91 us -> 7.7 us  [on_device(): pl.pallas_call(last_kernel, grid=(steps,), out_shape=(out(L, blk), out(T,...]
    pallas_call x1, Pallas kernels: 115 us -> 107 us  [on_device(): pl.pallas_call(functools.partial(kernel, (nc, nh, ny, tc)), out_shape=(ou...]
where the time goes in v2:
time: 117 us; the launch traced here: 115 us
  Pallas kernels  115 us (98%)
    pallas_call x1, Pallas kernels, on_device(): pl.pallas_call(functools.partial(kernel, (nc, nh, ny, tc)), out_shape=(ou...  107 us
    pallas_call x1, Pallas kernels, on_device(): pl.pallas_call(last_kernel, grid=(steps,), out_shape=(out(L, blk), out(T,...  7.7 us

profile of v2, /device:TPU:8, one launch (start us, length us, event | category | flops | bytes accessed | tf_op | source)
XLA Modules:
  0.0 115.3 jit_solution(18398587388286421346)
XLA Ops:
  0.6 107.0 %shard_map.118 = (f32[4,2,64,256]{3,2,1,0:T(8,128)}, f32[2048,256]{1,0:T(8,128)}, f32[4,2,64,256]{3,2,1,0:T(8,128)}, f32[128,512]{1,0:T(8,128)}, f32[4,2,64,256]{3,2,1,0:T(8,128)}) custom-call(f32[512,1024]{1,0:T(8,128)} %lat.3, f32[2048,1024]{1,0:T(8,128)} %obs.1, f32[1024,256]{1,0:T(8,128)} %wq.1, f32[1024,256]{1,0:T(8,128)} %wk.1, f32[1024,256]{1,0:T(8,128)} %wv.1, ...), custom_call_target="tpu_custom_call" | custom-call | flops 32999999488 | bytes 41943040 | tf_op jit(solution)/shard_map/pallas_call | solution.py:464
  107.6 7.7 %shard_map.119 = (f32[512,256]{1,0:T(8,128)}, f32[2048,256]{1,0:T(8,128)}, f32[1024,256]{1,0:T(8,128)}, f32[128,256]{1,0:T(8,128)}, f32[128,256]{1,0:T(8,128)}, /*index=5*/f32[256,1024]{1,0:T(8,128)}) custom-call(f32[512,256]{1,0:T(8,128)} %bitcast.5, f32[512,256]{1,0:T(8,128)} %bitcast.4, f32[512,1024]{1,0:T(8,128)} %lat.3, f32[512,1024]{1,0:T(8,128)} %dout.3, ...), custom_call_target="tpu_custom_call" | custom-call | flops 1610612736 | bytes 20971520 | tf_op jit(solution)/shard_map/pallas_call | solution.py:501
